TPU v7x, 128 devices: a whole 4x4x4 slice. The times are simulated.
128 devices in a mesh: rep: 64 (over y, x, z_lo, core), fsdp: 2 (over z_hi).
Axes of the slice: x: 4, y: 4, z: 4 (z_hi: 2, z_lo: 2; z = z_hi * 2 + z_lo), core: 2. Of those that a mesh axis runs over, the one named last changes fastest.
Arguments:
- tokens: bfloat16 [65536, 768], P(('rep', 'fsdp')), may hold values from -6 to 6
- norm_gain_one: bfloat16 [768], P('fsdp'), may hold values from 0.099609375 to 1.8984375
- qkv_weight: bfloat16 [768, 2304], P('fsdp'), may hold values from -0.21875 to 0.21875
- attn_out_weight: bfloat16 [768, 768], P('fsdp'), may hold values from -2.5 to 2.5
- norm_gain_two: bfloat16 [768], P('fsdp'), may hold values from 0.099609375 to 1.8984375
- in_weight: bfloat16 [768, 2304], P('fsdp'), may hold values from -0.21875 to 0.21875
- mlp_out_weight: bfloat16 [1152, 768], P('fsdp'), may hold values from -0.25 to 0.25
- cotangent: bfloat16 [65536, 768], P(('rep', 'fsdp')), may hold values from -6 to 6
Outputs:
- layer_output: bfloat16 [65536, 768], P(('rep', 'fsdp'))
- token_grad: bfloat16 [65536, 768], P(('rep', 'fsdp'))
- gain_one_grad: float32 [768], P('fsdp')
- qkv_grad: float32 [768, 2304], P('fsdp')
- attn_out_grad: float32 [768, 768], P('fsdp')
- gain_two_grad: float32 [768], P('fsdp')
- in_grad: float32 [768, 2304], P('fsdp')
- mlp_out_grad: float32 [1152, 768], P('fsdp')
All inputs are finite; a program needn't handle non-finite values.
Results may differ from a plain program's by a relative error of at most 0.018.
Values may be sent and summed in bfloat16 or wider, within the bound.
No kernel may reach another device: no remote copies, remote signals or barrier semaphores. Data moves between devices by JAX's collectives and lax.ppermute only.
A program may use at most 128 MiB of HBM per device.

v0:
```python
from functools import partial

import jax
import jax.numpy as jnp
from jax import lax
from jax.sharding import PartitionSpec as P

HEADS = 12
HEAD_DIM = 64
FF = 1152
HALF_WIN = 64


eps_norm = 1e-05
theta = 10000.0
masked_value = -1e30


def with_halo(x, sides, width):
    for axis, dim in sides:
        peers, length = (lax.axis_size(axis), x.shape[dim])
        up = [(i, (i + 1) % peers) for i in range(peers - 1)]
        down = [(j, i) for i, j in up]
        last = lax.slice_in_dim(x, length - width, length, axis=dim)
        first = lax.slice_in_dim(x, 0, width, axis=dim)
        before = lax.ppermute(last, axis, up)
        after = lax.ppermute(first, axis, down)
        x = jnp.concatenate([before, x, after], axis=dim)
    return x


def from_behind(x, axis, by):
    peers = lax.axis_size(axis)
    pairs = [(i, i + by) for i in range(peers) if 0 <= i + by < peers]
    return lax.ppermute(x, axis, pairs)


def layer_norm(values, gain):
    row_mean = jnp.mean(values, axis=-1, keepdims=True)
    centred = values - row_mean
    variance = jnp.mean(centred * centred, axis=-1, keepdims=True)
    return centred * lax.rsqrt(variance + eps_norm) * gain


def rotary(values, positions):
    half_dim = values.shape[-1] // 2
    frequency = theta ** (-(jnp.arange(half_dim, dtype=jnp.float32) * 2.0 / values.shape[-1]))
    angles = positions.astype(jnp.float32)[:, None] * frequency[None, :]
    cosine = jnp.concatenate([jnp.cos(angles), jnp.cos(angles)], -1)[:, None, :]
    sine = jnp.concatenate([jnp.sin(angles), jnp.sin(angles)], -1)[:, None, :]
    first_half = values[..., :half_dim]
    second = values[..., half_dim:]
    turned = jnp.concatenate([-second, first_half], -1)
    return values * cosine + turned * sine


def gelu_exact(values):
    return 0.5 * values * (1.0 + lax.erf(values * 0.7071067811865476))


def gated(up_proj, inner):
    return gelu_exact(up_proj[:, :inner]) * up_proj[:, inner:]


def windows(extended_part, blocks, tile):
    tiles = extended_part.reshape(blocks + 1, tile, HEADS, HEAD_DIM)
    return jnp.concatenate([tiles[:-1], tiles[1:]], 1)


def fold_windows(windowed, blocks, tile, width):
    flat = windowed.reshape(blocks, 2 * tile, width)
    first_part = flat[:, :tile].reshape(blocks * tile, width)
    second_part = flat[:, tile:].reshape(blocks * tile, width)
    return jnp.pad(first_part, ((0, tile), (0, 0))) + jnp.pad(second_part, ((tile, 0), (0, 0)))


def local(
    tokens,
    norm_gain_one,
    qkv_weight,
    attn_out_weight,
    norm_gain_two,
    in_weight,
    mlp_out_weight,
    cotangent,
):
    rows, width = tokens.shape
    shard_count = lax.axis_size("fsdp")
    seq_len = rows * shard_count
    base_pos = lax.axis_index("fsdp") * rows
    positions = base_pos + jnp.arange(rows, dtype=jnp.int32)
    score_scale = HEAD_DIM ** (-0.5)
    tile = 2 * HALF_WIN
    blocks = rows // tile
    full_gain_one, full_qkv, full_attn = (
        lax.all_gather(norm_gain_one, "fsdp", axis=0, tiled=True),
        lax.all_gather(qkv_weight, "fsdp", axis=0, tiled=True),
        lax.all_gather(attn_out_weight, "fsdp", axis=0, tiled=True),
    )
    inputs = tokens.astype(jnp.float32)
    normed_one, norm_one_pull = jax.vjp(layer_norm, inputs, full_gain_one.astype(jnp.float32))
    normed_one_b = normed_one.astype(jnp.bfloat16)
    projected = jnp.dot(normed_one_b, full_qkv, preferred_element_type=jnp.float32).reshape(
        rows, 3, HEADS, HEAD_DIM
    )

    def rope_pair(raw_query, raw_key):
        return (rotary(raw_query, positions), rotary(raw_key, positions))

    (rot_query, rot_key), rope_pull = jax.vjp(rope_pair, projected[:, 0], projected[:, 1])
    queries = rot_query.astype(jnp.bfloat16)
    query_tiles = queries.reshape(blocks, tile, HEADS, HEAD_DIM)
    keys_vals = jnp.concatenate(
        [rot_key.reshape(rows, width), projected[:, 2].reshape(rows, width)], 1
    ).astype(jnp.bfloat16)
    extended = with_halo(keys_vals, (("fsdp", 0),), HALF_WIN)
    win_keys = windows(extended[:, :width], blocks, tile)
    win_vals = windows(extended[:, width:], blocks, tile)
    local_query = jnp.arange(tile, dtype=jnp.int32)
    local_key = jnp.arange(2 * tile, dtype=jnp.int32)
    block_start = base_pos + jnp.arange(blocks, dtype=jnp.int32) * tile
    key_pos = block_start[:, None] - HALF_WIN + local_key[None, :]
    band = jnp.abs(local_query[:, None] - local_key[None, :] + HALF_WIN) <= HALF_WIN
    inside = (key_pos >= 0) & (key_pos < seq_len)
    allowed = (band[None, :, :] & inside[:, None, :])[:, None]

    def masked_scores():
        raw_scores = (
            jnp.einsum("bqhd,bkhd->bhqk", query_tiles, win_keys, preferred_element_type=jnp.float32)
            * score_scale
        )
        return jnp.where(allowed, raw_scores, masked_value)

    scores = masked_scores()
    top_score = jnp.max(scores, axis=-1, keepdims=True)
    log_total = top_score + jnp.log(jnp.sum(jnp.exp(scores - top_score), axis=-1, keepdims=True))
    probs_b = jnp.exp(scores - log_total).astype(jnp.bfloat16)
    attended = jnp.einsum("bhqk,bkhd->bqhd", probs_b, win_vals, preferred_element_type=jnp.float32)
    attended_b = attended.reshape(rows, width).astype(jnp.bfloat16)
    hidden = inputs + jnp.dot(attended_b, full_attn, preferred_element_type=jnp.float32)
    full_gain_two, full_in, full_mlp = (
        lax.all_gather(norm_gain_two, "fsdp", axis=0, tiled=True),
        lax.all_gather(in_weight, "fsdp", axis=0, tiled=True),
        lax.all_gather(mlp_out_weight, "fsdp", axis=0, tiled=True),
    )
    normed_two, norm_two_pull = jax.vjp(layer_norm, hidden, full_gain_two.astype(jnp.float32))
    normed_two_b = normed_two.astype(jnp.bfloat16)
    up_proj = jnp.dot(normed_two_b, full_in, preferred_element_type=jnp.float32)
    mixed, gate_pull = jax.vjp(partial(gated, inner=FF), up_proj)
    mixed_b = mixed.astype(jnp.bfloat16)
    output = hidden + jnp.dot(mixed_b, full_mlp, preferred_element_type=jnp.float32)
    layer_output = output.astype(jnp.bfloat16)
    back_in, back_mlp = (
        lax.all_gather(in_weight, "fsdp", axis=0, tiled=True),
        lax.all_gather(mlp_out_weight, "fsdp", axis=0, tiled=True),
    )
    back_qkv, back_attn = (
        lax.all_gather(qkv_weight, "fsdp", axis=0, tiled=True),
        lax.all_gather(attn_out_weight, "fsdp", axis=0, tiled=True),
    )
    grad_out = cotangent.astype(jnp.float32)
    mlp_out_full = jnp.einsum("tf,td->fd", mixed_b, cotangent, preferred_element_type=jnp.float32)
    d_mixed = jnp.einsum("td,fd->tf", cotangent, back_mlp, preferred_element_type=jnp.float32)
    (d_up,) = gate_pull(d_mixed)
    d_up_b = d_up.astype(jnp.bfloat16)
    in_full = jnp.einsum("td,tf->df", normed_two_b, d_up_b, preferred_element_type=jnp.float32)
    d_normed_two = jnp.einsum("tf,df->td", d_up_b, back_in, preferred_element_type=jnp.float32)
    d_hidden_norm, gain_two_full = norm_two_pull(d_normed_two)
    d_hidden = grad_out + d_hidden_norm
    mlp_shares = (
        lax.psum_scatter(
            gain_two_full.astype(jnp.bfloat16), "fsdp", scatter_dimension=0, tiled=True
        ).astype(jnp.float32),
        lax.psum_scatter(
            in_full.astype(jnp.bfloat16), "fsdp", scatter_dimension=0, tiled=True
        ).astype(jnp.float32),
        lax.psum_scatter(
            mlp_out_full.astype(jnp.bfloat16), "fsdp", scatter_dimension=0, tiled=True
        ).astype(jnp.float32),
    )
    d_branch_b = d_hidden.astype(jnp.bfloat16)
    attn_out_full = jnp.einsum(
        "tc,td->cd", attended_b, d_branch_b, preferred_element_type=jnp.float32
    )
    d_attended = jnp.einsum("td,cd->tc", d_branch_b, back_attn, preferred_element_type=jnp.float32)
    d_attended_b = d_attended.astype(jnp.bfloat16).reshape(blocks, tile, HEADS, HEAD_DIM)
    probs = jnp.exp(masked_scores() - log_total)
    d_probs = jnp.einsum(
        "bqhd,bkhd->bhqk", d_attended_b, win_vals, preferred_element_type=jnp.float32
    )
    row_delta = jnp.sum(probs * d_probs, axis=-1, keepdims=True)
    d_scores_b = (probs * (d_probs - row_delta)).astype(jnp.bfloat16)
    d_queries = (
        jnp.einsum("bhqk,bkhd->bqhd", d_scores_b, win_keys, preferred_element_type=jnp.float32)
        * score_scale
    )
    d_queries = d_queries.reshape(rows, HEADS, HEAD_DIM)
    d_win_keys = (
        jnp.einsum("bhqk,bqhd->bkhd", d_scores_b, query_tiles, preferred_element_type=jnp.float32)
        * score_scale
    )
    d_win_vals = jnp.einsum(
        "bhqk,bqhd->bkhd", probs_b, d_attended_b, preferred_element_type=jnp.float32
    )
    d_extended = jnp.concatenate(
        [
            fold_windows(d_win_keys, blocks, tile, width),
            fold_windows(d_win_vals, blocks, tile, width),
        ],
        1,
    )
    from_upper = from_behind(d_extended[:HALF_WIN].astype(jnp.bfloat16), "fsdp", -1).astype(
        jnp.float32
    )
    from_lower = from_behind(d_extended[rows + HALF_WIN :].astype(jnp.bfloat16), "fsdp", 1).astype(
        jnp.float32
    )
    d_owned = d_extended[HALF_WIN : HALF_WIN + rows]
    d_owned = (
        d_owned
        + jnp.pad(from_upper, ((rows - HALF_WIN, 0), (0, 0)))
        + jnp.pad(from_lower, ((0, rows - HALF_WIN), (0, 0)))
    )
    d_rot_key = d_owned[:, :width].reshape(rows, HEADS, HEAD_DIM)
    d_raw_value = d_owned[:, width:].reshape(rows, HEADS, HEAD_DIM)
    d_raw_query, d_raw_key = rope_pull((d_queries, d_rot_key))
    d_projected_b = (
        jnp.stack([d_raw_query, d_raw_key, d_raw_value], 1)
        .reshape(rows, 3 * width)
        .astype(jnp.bfloat16)
    )
    qkv_full = jnp.einsum(
        "td,tc->dc", normed_one_b, d_projected_b, preferred_element_type=jnp.float32
    )
    d_normed_one = jnp.einsum(
        "tc,dc->td", d_projected_b, back_qkv, preferred_element_type=jnp.float32
    )
    d_input_norm, gain_one_full = norm_one_pull(d_normed_one)
    token_grad = (d_hidden + d_input_norm).astype(jnp.bfloat16)
    attn_shares = (
        lax.psum_scatter(
            gain_one_full.astype(jnp.bfloat16), "fsdp", scatter_dimension=0, tiled=True
        ).astype(jnp.float32),
        lax.psum_scatter(
            qkv_full.astype(jnp.bfloat16), "fsdp", scatter_dimension=0, tiled=True
        ).astype(jnp.float32),
        lax.psum_scatter(
            attn_out_full.astype(jnp.bfloat16), "fsdp", scatter_dimension=0, tiled=True
        ).astype(jnp.float32),
    )
    gain_one_sum, qkv_sum, attn_out_sum, gain_two_sum, in_sum, mlp_out_sum = lax.psum(
        (
            attn_shares[0],
            attn_shares[1],
            attn_shares[2],
            mlp_shares[0],
            mlp_shares[1],
            mlp_shares[2],
        ),
        "rep",
    )
    return (
        layer_output,
        token_grad,
        gain_one_sum,
        qkv_sum,
        attn_out_sum,
        gain_two_sum,
        in_sum,
        mlp_out_sum,
    )


def solution(mesh):
    return jax.shard_map(
        local,
        mesh=mesh,
        in_specs=(
            P(("rep", "fsdp"), None),
            P("fsdp"),
            P("fsdp", None),
            P("fsdp", None),
            P("fsdp"),
            P("fsdp", None),
            P("fsdp", None),
            P(("rep", "fsdp"), None),
        ),
        out_specs=(
            P(("rep", "fsdp"), None),
            P(("rep", "fsdp"), None),
            P("fsdp"),
            P("fsdp", None),
            P("fsdp", None),
            P("fsdp"),
            P("fsdp", None),
            P("fsdp", None),
        ),
        check_vma=False,
    )
```

profile of v0, /device:TPU:1, one launch (start us, length us, event | category | flops | bytes accessed | tf_op | source)
XLA Modules:
  0.0 702.6 jit_solution(6292611521115766479)
XLA Ops:
  10.2 6.1 all-gather
  16.4 4.7 all-gather.1
  24.0 42.5 %all-gather.7.cloned.1.call-done = bf16[768,2304]{1,0:T(8,128)(2,1)} async-done(((bf16[384,2304]{1,0:T(8,128)(2,1)}), bf16[768,2304]{1,0:T(8,128)(2,1)}) %all-gather.7.cloned.1.call-update) | async-done | bytes 3538960 | tf_op jit(solution)/shard_map/all_gather | solution.py:97
  66.5 4.2 fusion.54
  76.2 3.9 slice_negate_fusion.2
  88.3 6.0 collective-permute-start
  94.9 7.5 %collective-permute-done.1 = bf16[64,1536]{0,1:T(8,128)(2,1)S(1)} collective-permute-done((bf16[64,1536]{0,1:T(8,128)(2,1)S(1)}, bf16[64,1536]{0,1:T(8,128)(2,1)S(1)}, u32[]{:S(2)}, u32[]{:S(2)}) %collective-permute-start.1) | collective-permute-done | bytes 196640 | tf_op jit(solution)/shard_map/ppermute | solution.py:27
  102.4 5.3 pad_maximum_fusion.2
  132.3 17.1 %all-gather.11.cloned.1.call-done = bf16[768,2304]{1,0:T(8,128)(2,1)} async-done(((bf16[384,2304]{1,0:T(8,128)(2,1)}), bf16[768,2304]{1,0:T(8,128)(2,1)}) %all-gather.11.cloned.1.call-update) | async-done | bytes 3538960 | tf_op jit(solution)/shard_map/all_gather | solution.py:143
  149.5 6.8 fusion.57
  156.2 27.6 %all-gather.13.cloned.1.call-done = bf16[1152,768]{1,0:T(8,128)(2,1)} async-done(((bf16[576,768]{1,0:T(8,128)(2,1)}), bf16[1152,768]{1,0:T(8,128)(2,1)}) %all-gather.13.cloned.1.call-update) | async-done | bytes 1769488 | tf_op jit(solution)/shard_map/all_gather | solution.py:144
  183.8 6.4 fusion.29
  197.6 3.8 convolution_convert_fusion.2
  201.5 6.3 convolution_convert_fusion
  211.5 4.1 fusion.32
  222.0 6.4 multiply_reduce_fusion
  242.3 5.8 collective-permute-start.3
  249.3 5.9 collective-permute-done.2
  266.5 4.1 convolution_convert_fusion.1
  272.5 4.7 add_convert_fusion.3
  281.4 6.3 all-reduce.15
  290.8 24.9 %reduce-scatter.9.cloned.1.call-done = bf16[384,2304]{1,0:T(8,128)(2,1)} async-done(((bf16[768,2304]{1,0:T(8,128)(2,1)}), bf16[384,2304]{1,0:T(8,128)(2,1)}) %reduce-scatter.9.cloned.1.call-update) | async-done | bytes 1769488 | tf_op jit(solution)/shard_map/reduce_scatter | solution.py:174
  315.7 54.2 %reduce-scatter.5.cloned.1.call-done = bf16[384,2304]{1,0:T(8,128)(2,1)} async-done(((bf16[768,2304]{1,0:T(8,128)(2,1)}), bf16[384,2304]{1,0:T(8,128)(2,1)}) %reduce-scatter.5.cloned.1.call-update) | async-done | bytes 1769488 | tf_op jit(solution)/shard_map/reduce_scatter | solution.py:244
  369.9 325.4 %all-reduce.17 = (f32[384]{0:T(512)}, f32[384,2304]{1,0:T(8,128)}, f32[384,768]{1,0:T(8,128)}, f32[384]{0:T(512)}, f32[384,2304]{1,0:T(8,128)}, /*index=5*/f32[576,768]{1,0:T(8,128)}) all-reduce(f32[384]{0:T(512)S(1)} %dynamic-slice_convert_fusion.1, ...), channel_id=1, replica_groups=mesh['rep'=64,'fsdp'=2] {'rep'}, use_global_device_ids=true, to_apply=%region_13.14 | all-reduce | flops 2507520 | bytes 15046656 | tf_op jit(solution)/shard_map/psum | solution.py:251
  (207 shorter events, 96.6 us)
Async XLA Ops:
  7.2 59.3 %all-gather.7.cloned.1.call-start = ((), (), s32[]{:S(2)}) async-start(), calls=%async_computation.4 | async-start | bytes 5308416 | tf_op jit(solution)/shard_map/all_gather | solution.py:97
  7.9 8.5 %copy-start.40 = (bf16[384]{0:T(512)(128)(2,1)S(1)}, bf16[384]{0:T(512)(128)(2,1)}, u32[]{:S(2)}) copy-start(bf16[384]{0:T(512)(128)(2,1)} %param.12) | copy-start | bytes 2308
  7.9 13.8 %copy-start.5 = (bf16[512,768]{1,0:T(8,128)(2,1)S(1)}, bf16[512,768]{1,0:T(8,128)(2,1)}, u32[]{:S(2)}) copy-start(bf16[512,768]{1,0:T(8,128)(2,1)} %param.8) | copy-start | bytes 2359300
  7.9 120.5 %all-gather.9.cloned.1.call-start = ((), (), s32[]{:S(2)}) async-start(), calls=%async_computation.5 | async-start | bytes 1769472 | tf_op jit(solution)/shard_map/all_gather | solution.py:98
  8.7 140.8 %all-gather.11.cloned.1.call-start = ((), (), s32[]{:S(2)}) async-start(), calls=%async_computation.6 | async-start | bytes 5308416 | tf_op jit(solution)/shard_map/all_gather | solution.py:143
  9.4 174.4 %all-gather.13.cloned.1.call-start = ((), (), s32[]{:S(2)}) async-start(), calls=%async_computation.7 | async-start | bytes 2654208 | tf_op jit(solution)/shard_map/all_gather | solution.py:144
  10.0 280.8 %reduce-scatter.7.cloned.1.call-start = ((), (), s32[]{:S(2)}) async-start(), calls=%async_computation.9 | async-start | bytes 1769472 | tf_op jit(solution)/shard_map/reduce_scatter | solution.py:247
  86.2 8.1 %copy-start.22 = (f32[4,128,12,32]{1,0,3,2:T(4,128)S(1)}, f32[4,128,12,32]{1,0,3,2:T(4,128)}, u32[]{:S(2)}) copy-start(f32[4,128,12,32]{1,0,3,2:T(4,128)} %concatenate.56) | copy-start | bytes 2359300
  86.2 8.1 %copy-start.33 = (f32[4,128,64]{1,0,2:T(4,128)S(1)}, f32[4,128,64]{1,0,2:T(4,128)}, u32[]{:S(2)}) copy-start(f32[4,128,64]{1,0,2:T(4,128)} %get-tuple-element.72) | copy-start | bytes 393220
  86.2 8.1 %copy-start.34 = (f32[4,128,64]{1,0,2:T(4,128)S(1)}, f32[4,128,64]{1,0,2:T(4,128)}, u32[]{:S(2)}) copy-start(f32[4,128,64]{1,0,2:T(4,128)} %get-tuple-element.73) | copy-start | bytes 393220
  86.6 7.7 %copy-start.13 = (f32[4,128,12,64]{1,0,3,2:T(4,128)S(1)}, f32[4,128,12,64]{1,0,3,2:T(4,128)}, u32[]{:S(2)}) copy-start(f32[4,128,12,64]{1,0,3,2:T(4,128)} %squeeze.12) | copy-start | bytes 4718596
  86.9 15.5 %collective-permute-start.1 = (bf16[64,1536]{0,1:T(8,128)(2,1)S(1)}, bf16[64,1536]{0,1:T(8,128)(2,1)S(1)}, u32[]{:S(2)}, u32[]{:S(2)}) collective-permute-start(bf16[64,1536]{0,1:T(8,128)(2,1)S(1)} %get-tuple-element.47), channel_id=1, source_target_pairs={{1,0},{3,2},{5,4},{7,6},{9,8},{11,10},{13,12},{15,14},{17,16},{19,... | collective-permute-start | bytes 589832 | tf_op jit(solution)/shard_map/ppermute | solution.py:27
  88.3 14.1 %collective-permute-start = (bf16[64,1536]{0,1:T(8,128)(2,1)S(1)}, bf16[64,1536]{0,1:T(8,128)(2,1)S(1)}, u32[]{:S(2)}, u32[]{:S(2)}) collective-permute-start(bf16[64,1536]{0,1:T(8,128)(2,1)S(1)} %get-tuple-element.48), channel_id=1, source_target_pairs={{0,1},{2,3},{4,5},{6,7},{8,9},{10,11},{12,13},{14,15},{16,17},{18,... | collective-permute-start | bytes 589832 | tf_op jit(solution)/shard_map/ppermute | solution.py:26
  130.9 18.6 %copy-start.37 = (f32[768]{0:T(1024)S(1)}, f32[768]{0:T(1024)}, u32[]{:S(2)}) copy-start(f32[768]{0:T(1024)} %reshape.242) | copy-start | bytes 9220
  156.2 34.0 %copy-start.11 = (f32[512,768]{1,0:T(8,128)S(1)}, f32[512,768]{1,0:T(8,128)}, u32[]{:S(2)}) copy-start(f32[512,768]{1,0:T(8,128)} %copy-done.10) | copy-start | bytes 4718596
  197.5 93.3 %reduce-scatter.11.cloned.1.call-start = ((), (), s32[]{:S(2)}) async-start(), calls=%async_computation.11 | async-start | bytes 2654208 | tf_op jit(solution)/shard_map/reduce_scatter | solution.py:177
  201.4 114.3 %reduce-scatter.9.cloned.1.call-start = ((), (), s32[]{:S(2)}) async-start(), calls=%async_computation.10 | async-start | bytes 5308416 | tf_op jit(solution)/shard_map/reduce_scatter | solution.py:174
  207.9 162.0 %reduce-scatter.5.cloned.1.call-start = ((), (), s32[]{:S(2)}) async-start(), calls=%async_computation.8 | async-start | bytes 5308416 | tf_op jit(solution)/shard_map/reduce_scatter | solution.py:244
  218.7 9.7 %slice-start = ((s8[6291456]{0:T(1024)(128)(4,1)}), s8[2097152]{0:T(1024)(128)(4,1)S(1)}, s32[]{:S(2)}) async-start(s8[6291456]{0:T(1024)(128)(4,1)} %bitcast.101), calls=%async_computation.12 | async-start | bytes 4194304
  240.7 14.5 %collective-permute-start.2 = (bf16[64,1536]{1,0:T(8,128)(2,1)S(1)}, bf16[64,1536]{1,0:T(8,128)(2,1)S(1)}, u32[]{:S(2)}, u32[]{:S(2)}) collective-permute-start(bf16[64,1536]{1,0:T(8,128)(2,1)S(1)} %get-tuple-element.33), channel_id=1, source_target_pairs={{1,0},{3,2},{5,4},{7,6},{9,8},{11,10},{13,12},{15,14},{17,16},{19,... | collective-permute-start | bytes 589832 | tf_op jit(solution)/shard_map/ppermute | solution.py:35
  242.3 13.8 %collective-permute-start.3 = (bf16[64,1536]{1,0:T(8,128)(2,1)S(1)}, bf16[64,1536]{1,0:T(8,128)(2,1)S(1)}, u32[]{:S(2)}, u32[]{:S(2)}) collective-permute-start(bf16[64,1536]{1,0:T(8,128)(2,1)S(1)} %get-tuple-element.34), channel_id=1, source_target_pairs={{0,1},{2,3},{4,5},{6,7},{8,9},{10,11},{12,13},{14,15},{16,17},{18,... | collective-permute-start | bytes 589832 | tf_op jit(solution)/shard_map/ppermute | solution.py:35
  279.4 8.4 %copy-start.4 = (f32[512,768]{1,0:T(8,128)S(1)}, f32[512,768]{1,0:T(8,128)}, u32[]{:S(2)}) copy-start(f32[512,768]{1,0:T(8,128)} %copy-done.3) | copy-start | bytes 4718596
  279.5 8.4 %copy-start.26 = (bf16[512,768]{1,0:T(8,128)(2,1)S(1)}, bf16[512,768]{1,0:T(8,128)(2,1)}, u32[]{:S(2)}) copy-start(bf16[512,768]{1,0:T(8,128)(2,1)} %param.15) | copy-start | bytes 2359300
  279.5 8.4 %copy-start.36 = (f32[512]{0:T(512)S(1)}, f32[512]{0:T(512)}, u32[]{:S(2)}) copy-start(f32[512]{0:T(512)} %copy-done.35) | copy-start | bytes 6148
  (36 other events, 100.0 us)
Sparse Core Ops, SparseCore 0:
  9.7 56.7 all-gather.6
  68.1 26.8 all-gather.8
  96.6 52.7 all-gather.10
  151.0 32.7 all-gather.12
  197.7 25.1 reduce-scatter.6
  225.8 35.8 reduce-scatter.10
  264.6 51.1 reduce-scatter.8
  318.8 51.0 reduce-scatter.4
where the time goes:
time: 714 us; the launch traced here: 703 us
  blocking collectives  342 us (48%)
  waiting for transfers between devices  183 us (26%)
  matrix products  64 us (9%)
  local copies, waits for them, and re-layouts  54.8 us (8%)
  other arithmetic  26.7 us (4%)
  between operations  16.1 us (2%)
  starting transfers between devices  15.3 us (2%)
    psum x1, blocking collectives, local(): lax.psum((attn_shares[0], attn_shares[1], attn_shares[2], mlp_shares[0],...  325 us
    reduce_scatter x1, waiting for transfers between devices, local(): lax.psum_scatter(qkv_full.astype(jnp.bfloat16), 'fsdp', scatter_dimension...  54.2 us
    all_gather x1, waiting for transfers between devices, local(): lax.all_gather(qkv_weight, 'fsdp', axis=0, tiled=True)  42.5 us
    all_gather x1, waiting for transfers between devices, local(): lax.all_gather(mlp_out_weight, 'fsdp', axis=0, tiled=True)  27.6 us
    reduce_scatter x1, waiting for transfers between devices, local(): lax.psum_scatter(in_full.astype(jnp.bfloat16), 'fsdp', scatter_dimension=...  24.9 us
    unnamed x105, local copies, waits for them, and re-layouts  24.2 us
    all_gather x1, waiting for transfers between devices, local(): lax.all_gather(in_weight, 'fsdp', axis=0, tiled=True)  17.1 us
  transfers between devices with their start and end apart: 12, of which 8 were waited for; matrix products, arithmetic and copies ran while one was open for 18% of the time, Pallas kernels for 0%

commit v1 on v0

--- a/solution.py
+++ b/solution.py
@@ -29,10 +29,119 @@
     return x
 
 
+YAXIS, XAXIS, NEAR, CORE, FAR = "y", "x", "zl", "c", "zh"
+PAIRS_A = [(0, 1), (1, 0), (2, 3), (3, 2)]
+PAIRS_B = [(0, 3), (3, 0), (1, 2), (2, 1)]
+SWAP = [(0, 1), (1, 0)]
+
+
+def by_core(axis, even, odd):
+    return [
+        (i * 2 + c, j * 2 + c) for c, pairs in ((0, even), (1, odd)) for i, j in pairs
+    ]
+
+
+def ring_swap(x, axis, first):
+    even, odd = (PAIRS_A, PAIRS_B) if first else (PAIRS_B, PAIRS_A)
+    if axis == YAXIS:
+        pairs = [
+            ((i * 4 + k) * 4 + r, (j * 4 + k) * 4 + r)
+            for z in range(2)
+            for c, group in ((0, even), (1, odd))
+            for r in (z * 2 + c,)
+            for k in range(4)
+            for i, j in group
+        ]
+        return lax.ppermute(x, (YAXIS, XAXIS, NEAR, CORE), pairs)
+    pairs = [
+        (i * 4 + z * 2 + c, j * 4 + z * 2 + c)
+        for z in range(2)
+        for c, group in ((0, even), (1, odd))
+        for i, j in group
+    ]
+    return lax.ppermute(x, (XAXIS, NEAR, CORE), pairs)
+
+
+def depth_swap(x, first):
+    across = [(i, 3 - i) for i in range(4)]
+    within = [(i, i ^ 2) for i in range(4)]
+    even, odd = (across, within) if first else (within, across)
+    pairs = []
+    for c, group in ((0, even), (1, odd)):
+        for i, j in group:
+            pairs.append(((i >> 1) * 4 + c * 2 + (i & 1), (j >> 1) * 4 + c * 2 + (j & 1)))
+    return lax.ppermute(x, (NEAR, CORE, FAR), pairs)
+
+
+def across_halves(x):
+    return lax.ppermute(x, (NEAR, FAR), [(i, 3 - i) for i in range(4)])
+
+
+def core_swap(x):
+    return lax.ppermute(x, CORE, SWAP)
+
+
+def pick(x, index, axis):
+    return lax.dynamic_index_in_dim(x, index, axis, keepdims=False)
+
+
+def ordered(mine, other, index, axis):
+    return jnp.where(index == 0, jnp.stack([mine, other], axis), jnp.stack([other, mine], axis))
+
+
+def add(a, b):
+    return (a.astype(jnp.float32) + b.astype(jnp.float32)).astype(jnp.bfloat16)
+
+
+def whole_rows(own):
+    rows, cols = own.shape
+    core, half = lax.axis_index(CORE), lax.axis_index(FAR)
+    piece = across_halves(pick(own.reshape(2, rows // 2, cols), core, 0))
+    missing = ordered(piece, core_swap(piece), core, 0).reshape(rows, cols)
+    return ordered(own, missing, half, 0).reshape(2 * rows, cols)
+
+
+def total_rows(partial):
+    rows, cols = partial.shape
+    core, half = lax.axis_index(CORE), lax.axis_index(FAR)
+    near, xi, yi = lax.axis_index(NEAR), lax.axis_index(XAXIS), lax.axis_index(YAXIS)
+    first_bit = lambda i: jnp.where(core == 0, ((i + 1) >> 1) & 1, i >> 1)
+    second_bit = lambda i: i & 1
+    near = near ^ half
+    data = partial.astype(jnp.bfloat16).reshape(2, 2, 2, 2, rows // 16, 2, cols // 2)
+    data = jnp.moveaxis(data, 5, 0)
+    data = add(pick(data, core, 0), core_swap(pick(data, 1 - core, 0)))
+    bit = first_bit(xi)
+    data = add(pick(data, bit, 1), ring_swap(pick(data, 1 - bit, 1), XAXIS, True))
+    bit = second_bit(xi)
+    data = add(pick(data, bit, 1), ring_swap(pick(data, 1 - bit, 1), XAXIS, False))
+    data = jnp.where(core == 0, data, jnp.swapaxes(data, 0, 1))
+    bit = jnp.where(core == 0, half, near)
+    data = add(pick(data, bit, 0), depth_swap(pick(data, 1 - bit, 0), True))
+    bit = jnp.where(core == 0, near, half)
+    data = add(pick(data, bit, 0), depth_swap(pick(data, 1 - bit, 0), False))
+    data = add(data, ring_swap(data, YAXIS, True))
+    data = add(data, ring_swap(data, YAXIS, False))
+    data = ordered(data, lax.ppermute(data, NEAR, SWAP), near, 0)
+    data = ordered(data, ring_swap(data, XAXIS, False), second_bit(xi), 0)
+    data = ordered(data, ring_swap(data, XAXIS, True), first_bit(xi), 0)
+    data = ordered(data, core_swap(data), core, 4)
+    return data.reshape(rows // 2, cols).astype(jnp.float32)
+
+
 def from_behind(x, axis, by):
     peers = lax.axis_size(axis)
     pairs = [(i, i + by) for i in range(peers) if 0 <= i + by < peers]
     return lax.ppermute(x, axis, pairs)
+
+
+def whole_gain(own):
+    half = lax.axis_index(FAR)
+    return ordered(own, across_halves(own), half, 0).reshape(-1)
+
+
+def gain_total(weight_sum, weight, gain):
+    return jnp.sum(weight_sum * weight.astype(jnp.float32), axis=-1) / gain.astype(jnp.float32)
 
 
 def layer_norm(values, gain):
@@ -85,18 +194,17 @@
     cotangent,
 ):
     rows, width = tokens.shape
-    shard_count = lax.axis_size("fsdp")
+    shard_count = lax.axis_size(FAR)
     seq_len = rows * shard_count
-    base_pos = lax.axis_index("fsdp") * rows
+    base_pos = lax.axis_index(FAR) * rows
     positions = base_pos + jnp.arange(rows, dtype=jnp.int32)
     score_scale = HEAD_DIM ** (-0.5)
     tile = 2 * HALF_WIN
     blocks = rows // tile
-    full_gain_one, full_qkv, full_attn = (
-        lax.all_gather(norm_gain_one, "fsdp", axis=0, tiled=True),
-        lax.all_gather(qkv_weight, "fsdp", axis=0, tiled=True),
-        lax.all_gather(attn_out_weight, "fsdp", axis=0, tiled=True),
-    )
+    full_gain_one = whole_gain(norm_gain_one)
+    full_gain_two = whole_gain(norm_gain_two)
+    full_qkv, full_attn = whole_rows(qkv_weight), whole_rows(attn_out_weight)
+    full_in, full_mlp = whole_rows(in_weight), whole_rows(mlp_out_weight)
     inputs = tokens.astype(jnp.float32)
     normed_one, norm_one_pull = jax.vjp(layer_norm, inputs, full_gain_one.astype(jnp.float32))
     normed_one_b = normed_one.astype(jnp.bfloat16)
@@ -113,7 +221,7 @@
     keys_vals = jnp.concatenate(
         [rot_key.reshape(rows, width), projected[:, 2].reshape(rows, width)], 1
     ).astype(jnp.bfloat16)
-    extended = with_halo(keys_vals, (("fsdp", 0),), HALF_WIN)
+    extended = with_halo(keys_vals, ((FAR, 0),), HALF_WIN)
     win_keys = windows(extended[:, :width], blocks, tile)
     win_vals = windows(extended[:, width:], blocks, tile)
     local_query = jnp.arange(tile, dtype=jnp.int32)
@@ -138,11 +246,6 @@
     attended = jnp.einsum("bhqk,bkhd->bqhd", probs_b, win_vals, preferred_element_type=jnp.float32)
     attended_b = attended.reshape(rows, width).astype(jnp.bfloat16)
     hidden = inputs + jnp.dot(attended_b, full_attn, preferred_element_type=jnp.float32)
-    full_gain_two, full_in, full_mlp = (
-        lax.all_gather(norm_gain_two, "fsdp", axis=0, tiled=True),
-        lax.all_gather(in_weight, "fsdp", axis=0, tiled=True),
-        lax.all_gather(mlp_out_weight, "fsdp", axis=0, tiled=True),
-    )
     normed_two, norm_two_pull = jax.vjp(layer_norm, hidden, full_gain_two.astype(jnp.float32))
     normed_two_b = normed_two.astype(jnp.bfloat16)
     up_proj = jnp.dot(normed_two_b, full_in, preferred_element_type=jnp.float32)
@@ -150,14 +253,7 @@
     mixed_b = mixed.astype(jnp.bfloat16)
     output = hidden + jnp.dot(mixed_b, full_mlp, preferred_element_type=jnp.float32)
     layer_output = output.astype(jnp.bfloat16)
-    back_in, back_mlp = (
-        lax.all_gather(in_weight, "fsdp", axis=0, tiled=True),
-        lax.all_gather(mlp_out_weight, "fsdp", axis=0, tiled=True),
-    )
-    back_qkv, back_attn = (
-        lax.all_gather(qkv_weight, "fsdp", axis=0, tiled=True),
-        lax.all_gather(attn_out_weight, "fsdp", axis=0, tiled=True),
-    )
+    back_in, back_mlp, back_qkv, back_attn = full_in, full_mlp, full_qkv, full_attn
     grad_out = cotangent.astype(jnp.float32)
     mlp_out_full = jnp.einsum("tf,td->fd", mixed_b, cotangent, preferred_element_type=jnp.float32)
     d_mixed = jnp.einsum("td,fd->tf", cotangent, back_mlp, preferred_element_type=jnp.float32)
@@ -165,19 +261,9 @@
     d_up_b = d_up.astype(jnp.bfloat16)
     in_full = jnp.einsum("td,tf->df", normed_two_b, d_up_b, preferred_element_type=jnp.float32)
     d_normed_two = jnp.einsum("tf,df->td", d_up_b, back_in, preferred_element_type=jnp.float32)
-    d_hidden_norm, gain_two_full = norm_two_pull(d_normed_two)
+    d_hidden_norm, _ = norm_two_pull(d_normed_two)
     d_hidden = grad_out + d_hidden_norm
-    mlp_shares = (
-        lax.psum_scatter(
-            gain_two_full.astype(jnp.bfloat16), "fsdp", scatter_dimension=0, tiled=True
-        ).astype(jnp.float32),
-        lax.psum_scatter(
-            in_full.astype(jnp.bfloat16), "fsdp", scatter_dimension=0, tiled=True
-        ).astype(jnp.float32),
-        lax.psum_scatter(
-            mlp_out_full.astype(jnp.bfloat16), "fsdp", scatter_dimension=0, tiled=True
-        ).astype(jnp.float32),
-    )
+    in_sum, mlp_out_sum = total_rows(in_full), total_rows(mlp_out_full)
     d_branch_b = d_hidden.astype(jnp.bfloat16)
     attn_out_full = jnp.einsum(
         "tc,td->cd", attended_b, d_branch_b, preferred_element_type=jnp.float32
@@ -209,10 +295,10 @@
         ],
         1,
     )
-    from_upper = from_behind(d_extended[:HALF_WIN].astype(jnp.bfloat16), "fsdp", -1).astype(
+    from_upper = from_behind(d_extended[:HALF_WIN].astype(jnp.bfloat16), FAR, -1).astype(
         jnp.float32
     )
-    from_lower = from_behind(d_extended[rows + HALF_WIN :].astype(jnp.bfloat16), "fsdp", 1).astype(
+    from_lower = from_behind(d_extended[rows + HALF_WIN :].astype(jnp.bfloat16), FAR, 1).astype(
         jnp.float32
     )
     d_owned = d_extended[HALF_WIN : HALF_WIN + rows]
@@ -235,30 +321,11 @@
     d_normed_one = jnp.einsum(
         "tc,dc->td", d_projected_b, back_qkv, preferred_element_type=jnp.float32
     )
-    d_input_norm, gain_one_full = norm_one_pull(d_normed_one)
+    d_input_norm, _ = norm_one_pull(d_normed_one)
     token_grad = (d_hidden + d_input_norm).astype(jnp.bfloat16)
-    attn_shares = (
-        lax.psum_scatter(
-            gain_one_full.astype(jnp.bfloat16), "fsdp", scatter_dimension=0, tiled=True
-        ).astype(jnp.float32),
-        lax.psum_scatter(
-            qkv_full.astype(jnp.bfloat16), "fsdp", scatter_dimension=0, tiled=True
-        ).astype(jnp.float32),
-        lax.psum_scatter(
-            attn_out_full.astype(jnp.bfloat16), "fsdp", scatter_dimension=0, tiled=True
-        ).astype(jnp.float32),
-    )
-    gain_one_sum, qkv_sum, attn_out_sum, gain_two_sum, in_sum, mlp_out_sum = lax.psum(
-        (
-            attn_shares[0],
-            attn_shares[1],
-            attn_shares[2],
-            mlp_shares[0],
-            mlp_shares[1],
-            mlp_shares[2],
-        ),
-        "rep",
-    )
+    attn_out_sum, qkv_sum = total_rows(attn_out_full), total_rows(qkv_full)
+    gain_one_sum = gain_total(qkv_sum, qkv_weight, norm_gain_one)
+    gain_two_sum = gain_total(in_sum, in_weight, norm_gain_two)
     return (
         layer_output,
         token_grad,
@@ -272,28 +339,14 @@
 
 
 def solution(mesh):
+    fine = jax.sharding.Mesh(
+        mesh.devices.reshape(4, 4, 2, 2, 2), (YAXIS, XAXIS, NEAR, CORE, FAR)
+    )
+    every = P((YAXIS, XAXIS, NEAR, CORE, FAR), None)
     return jax.shard_map(
         local,
-        mesh=mesh,
-        in_specs=(
-            P(("rep", "fsdp"), None),
-            P("fsdp"),
-            P("fsdp", None),
-            P("fsdp", None),
-            P("fsdp"),
-            P("fsdp", None),
-            P("fsdp", None),
-            P(("rep", "fsdp"), None),
-        ),
-        out_specs=(
-            P(("rep", "fsdp"), None),
-            P(("rep", "fsdp"), None),
-            P("fsdp"),
-            P("fsdp", None),
-            P("fsdp", None),
-            P("fsdp"),
-            P("fsdp", None),
-            P("fsdp", None),
-        ),
+        mesh=fine,
+        in_specs=(every, P(FAR), P(FAR, None), P(FAR, None), P(FAR), P(FAR, None), P(FAR, None), every),
+        out_specs=(every, every, P(FAR), P(FAR, None), P(FAR, None), P(FAR), P(FAR, None), P(FAR, None)),
         check_vma=False,
     )

time: 714 us -> 454 us (0.64)
  blocking collectives: 342 us -> 0 us
  starting transfers between devices: 15.3 us -> 110 us
  waiting for transfers between devices: 183 us -> 119 us
  local copies, waits for them, and re-layouts: 54.8 us -> 115 us
  other arithmetic: 26.7 us -> 51.3 us
  matrix products: 64 us -> 48.8 us
  between operations: 16.1 us -> 2.55 us
    psum x1 -> x0, blocking collectives: 325 us -> none  [local(): lax.psum((attn_shares[0], attn_shares[1], attn_shares[2], mlp_shares[0],...]
    ppermute x0 -> x54, waiting for transfers between devices: none -> 110 us  [the longest x16 43.7 us: ring_swap(): return lax.ppermute(x, (XAXIS, NEAR, CORE), pairs)]
    ppermute x0 -> x54, starting transfers between devices: none -> 95.3 us  [the longest x12 40.6 us: core_swap(): return lax.ppermute(x, CORE, SWAP)]
    all_gather x4 -> x0, waiting for transfers between devices: 87.2 us -> none  [the longest x1 42.5 us: local(): lax.all_gather(qkv_weight, 'fsdp', axis=0, tiled=True)]
    reduce_scatter x4 -> x0, waiting for transfers between devices: 79 us -> none  [the longest x1 54.2 us: local(): lax.psum_scatter(qkv_full.astype(jnp.bfloat16), 'fsdp', scatter_dimension...]
    another operation x0 -> x9, local copies, waits for them, and re-layouts: none -> 36.2 us
    reshape x0 -> x8, local copies, waits for them, and re-layouts: none -> 24.5 us  [the longest x4 21.3 us: total_rows(): partial.astype(jnp.bfloat16).reshape(2, 2, 2, 2, rows // 16, 2, cols // 2)]
    select_n x0 -> x36, other arithmetic: none -> 13.7 us  [the longest x32 13.6 us: ordered(): jnp.where(index == 0, jnp.stack([mine, other], axis), jnp.stack([other, m...]
  transfers between devices with their start and end apart: 12 -> 58, of which waited for: 8 -> 30; matrix products, arithmetic and copies ran while one was open for 18% -> 28% of each run, Pallas kernels for 0% -> 0%
where the time goes in v1:
time: 454 us; the launch traced here: 446 us
  waiting for transfers between devices  119 us (26%)
  local copies, waits for them, and re-layouts  115 us (25%)
  starting transfers between devices  110 us (24%)
  other arithmetic  51.3 us (11%)
  matrix products  48.8 us (11%)
    ppermute x16, waiting for transfers between devices, ring_swap(): return lax.ppermute(x, (XAXIS, NEAR, CORE), pairs)  43.7 us
    ppermute x12, starting transfers between devices, core_swap(): return lax.ppermute(x, CORE, SWAP)  40.6 us
    ppermute x6, waiting for transfers between devices, across_halves(): return lax.ppermute(x, (NEAR, FAR), [(i, 3 - i) for i in range(4)])  37.8 us
    another operation x5, local copies, waits for them, and re-layouts  36.2 us
    reshape x4, local copies, waits for them, and re-layouts, total_rows(): partial.astype(jnp.bfloat16).reshape(2, 2, 2, 2, rows // 16, 2, cols // 2)  21.3 us
    ppermute x16, starting transfers between devices, ring_swap(): return lax.ppermute(x, (XAXIS, NEAR, CORE), pairs)  18.4 us
    unnamed x133, local copies, waits for them, and re-layouts  17.5 us
    select_n x32, other arithmetic, ordered(): jnp.where(index == 0, jnp.stack([mine, other], axis), jnp.stack([other, m...  13.6 us
  transfers between devices with their start and end apart: 58, of which 30 were waited for; matrix products, arithmetic and copies ran while one was open for 28% of the time, Pallas kernels for 0%

profile of v1, /device:TPU:1, one launch (start us, length us, event | category | flops | bytes accessed | tf_op | source)
XLA Modules:
  0.0 445.6 jit_solution(10307831755035128038)
XLA Ops:
  0.6 4.7 %collective-permute-start = (bf16[384]{0:T(512)(128)(2,1)}, bf16[384]{0:T(512)(128)(2,1)S(1)}, u32[]{:S(2)}, u32[]{:S(2)}) collective-permute-start(bf16[384]{0:T(512)(128)(2,1)} %param.9), channel_id=1, source_target_pairs={{0,5},{1,4},{4,1},{5,0},{2,7},{3,6},{6,3},{7,2},{8,13},{9,12},{12,... | collective-permute-start | bytes 2312 | tf_op jit(solution)/shard_map/ppermute | solution.py:77
  20.7 23.8 %collective-permute-done.1 = bf16[192,2304]{1,0:T(8,128)(2,1)} collective-permute-done((bf16[192,2304]{1,0:T(8,128)(2,1)}, bf16[192,2304]{1,0:T(8,128)(2,1)}, u32[]{:S(2)}, u32[]{:S(2)}) %collective-permute-start.1) | collective-permute-done | bytes 884768 | tf_op jit(solution)/shard_map/ppermute | solution.py:77
  49.5 14.0 %collective-permute-done.7 = bf16[384]{0:T(512)(128)(2,1)S(1)} collective-permute-done((bf16[384]{0:T(512)(128)(2,1)S(1)}, bf16[384]{0:T(512)(128)(2,1)S(1)}, u32[]{:S(2)}, u32[]{:S(2)}) %collective-permute-start.7) | collective-permute-done | bytes 800 | tf_op jit(solution)/shard_map/ppermute | solution.py:77
  92.8 5.7 %collective-permute-start.3 = (bf16[64,1536]{0,1:T(8,128)(2,1)S(1)}, bf16[64,1536]{0,1:T(8,128)(2,1)S(1)}, u32[]{:S(2)}, u32[]{:S(2)}) collective-permute-start(bf16[64,1536]{0,1:T(8,128)(2,1)S(1)} %get-tuple-element.42), channel_id=1, source_target_pairs={{0,1},{2,3},{4,5},{6,7},{8,9},{10,11},{12,13},{14,15},{16,17},{18,... | collective-permute-start | bytes 589832 | tf_op jit(solution)/shard_map/ppermute | solution.py:26
  106.5 5.0 %pad_maximum_fusion.1 = (bf16[512,768]{0,1:T(8,128)(2,1)}, bf16[512,768]{0,1:T(8,128)(2,1)S(1)}, bf16[512,768]{0,1:T(8,128)(2,1)S(1)}, bf16[512,768]{0,1:T(8,128)(2,1)}) fusion(bf16[64,1536]{0,1:T(8,128)(2,1)S(1)} %collective-permute-done.4, bf16[512,768]{0,1:T(8,128)(2,1)S(1)} %bitcast.369, bf16[512,768]{0,1:T(8,128)(2,1)S(1)} %fusion.27, ...), kind=kLoop, calls=%fused_computation.132 | loop fusion | flops 9437184 | bytes 5111808 | tf_op jit(solution)/shard_map/concatenate | solution.py:28
  152.3 5.3 %fusion.43 = f32[4,12,64,256]{3,2,1,0:T(8,128)} fusion(bf16[4,128,12,64]{1,0,3,2:T(4,128)(2,1)S(1)} %reshape.1660, f32[4,12,128,256]{3,2,1,0:T(8,128)} %copy-done, f32[4,12,128]{2,1,0:T(8,128)S(1)} %log_add_fusion, pred[4,128,256]{2,1,0:T(8,128)(4,1)S(1)} %copy-done.29), kind=kOutput, calls=%fused_computation.152 | convolution fusion | flops 207618048 | bytes 10379264 | tf_op jit(solution)/shard_map/bhqk,bqhd->bkhd/dot_general | solution.py:288
  157.6 5.3 %multiply_reduce_fusion = (f32[4,12,128]{2,1,0:T(8,128)}, f32[4,12,128,256]{3,2,1,0:T(8,128)}) fusion(f32[4,12,128,256]{3,2,1,0:T(8,128)S(1)} %bitcast.348, f32[4,12,128]{2,1,0:T(8,128)S(1)} %log_add_fusion, pred[4,128,256]{2,1,0:T(8,128)(4,1)S(1)} %copy-done.29, bf16[4,256,12,64]{1,3,2,0:T(8,128)(2,1)S(1)} %copy-done.33, ...), kind=kOutput, calls=%fused_computation.1 | convolution fusion | flops 209184768 | bytes 15122432 | tf_op jit(solution)/shard_map/bqhd,bkhd->bhqk/dot_general | solution.py:274
  162.9 6.6 %reshape.1671 = bf16[2,2,2,2,48,2,1152]{6,5,4,3,2,1,0:T(2,128)(2,1)S(1)} reshape(bf16[768,2304]{1,0:T(8,128)(2,1)} %convolution_convert_fusion) | data formatting | bytes 7077888 | tf_op jit(solution)/shard_map/reshape | solution.py:111
  177.6 5.5 %constant_dynamic-slice_fusion.5 = (bf16[2,2,2,2,48,1,384]{6,5,4,3,2,1,0:T(2,128)(2,1)}, bf16[2,2,2,2,48,1,384]{6,5,4,3,2,1,0:T(2,128)(2,1)S(1)}) fusion(bf16[2,2,2,2,48,2,384]{6,5,4,3,2,1,0:T(2,128)(2,1)} %reshape.1670, s32[]{:T(128)S(6)} %select_n.604, s32[]{:T(128)S(6)} %select_n.633), kind=kLoop, calls=%fused_computation.249 | loop fusion | bytes 2359304 | tf_op jit(solution)/shard_map/dynamic-slice.2
  185.1 4.9 %constant_dynamic-slice_fusion.1 = (bf16[2,2,2,2,72,1,384]{6,5,4,3,2,1,0:T(2,128)(2,1)}, bf16[2,2,2,2,72,1,384]{6,5,4,3,2,1,0:T(2,128)(2,1)S(1)}) fusion(bf16[2,2,2,2,72,2,384]{6,5,4,3,2,1,0:T(2,128)(2,1)S(1)} %copy-done.1, s32[]{:T(128)S(6)} %select_n.604, s32[]{:T(128)S(6)} %select_n.633), kind=kLoop, calls=%fused_computation.245 | loop fusion | bytes 3538952 | tf_op jit(solution)/shard_map/dynamic-slice.6
  195.3 11.1 %constant_dynamic-slice_fusion.3 = (bf16[2,2,2,2,48,1,1152]{6,5,4,3,2,1,0:T(2,128)(2,1)}, bf16[2,2,2,2,48,1,1152]{6,5,4,3,2,1,0:T(2,128)(2,1)}) fusion(bf16[2,2,2,2,48,2,1152]{6,5,4,3,2,1,0:T(2,128)(2,1)S(1)} %reshape.1671, s32[]{:T(128)S(6)} %select_n.604, s32[]{:T(128)S(6)} %select_n.633), kind=kLoop, calls=%fused_computation.247 | loop fusion | bytes 7077896 | tf_op jit(solution)/shard_map/dynamic-slice.4
  210.0 6.0 %multiply_convert_fusion = bf16[4,12,128,256]{3,2,1,0:T(8,128)(2,1)S(1)} fusion(f32[4,12,128,256]{3,2,1,0:T(8,128)} %get-tuple-element.62, f32[4,12,128,256]{3,2,1,0:T(8,128)} %copy-done, f32[4,12,128]{2,1,0:T(8,128)S(1)} %copy-done.50, f32[4,12,128]{2,1,0:T(8,128)S(1)} %copy-done.49, pred[4,128,256]{2,1,0:T(8,128)(4,1)S(1)} %copy-done.30), kind=kLoop, calls=%fused_computation | loop fusion | flops 9437184 | bytes 15908864 | tf_op jit(solution)/shard_map/convert_element_type | solution.py:278
  221.3 5.8 %collective-permute-start.13 = (bf16[64,1536]{0,1:T(8,128)(2,1)S(1)}, bf16[64,1536]{0,1:T(8,128)(2,1)S(1)}, u32[]{:S(2)}, u32[]{:S(2)}) collective-permute-start(bf16[64,1536]{0,1:T(8,128)(2,1)S(1)} %get-tuple-element.26), channel_id=1, source_target_pairs={{0,1},{2,3},{4,5},{6,7},{8,9},{10,11},{12,13},{14,15},{16,17},{18,... | collective-permute-start | bytes 589832 | tf_op jit(solution)/shard_map/ppermute | solution.py:135
  228.4 5.5 %collective-permute-done.12 = bf16[64,1536]{0,1:T(8,128)(2,1)S(1)} collective-permute-done((bf16[64,1536]{0,1:T(8,128)(2,1)S(1)}, bf16[64,1536]{0,1:T(8,128)(2,1)S(1)}, u32[]{:S(2)}, u32[]{:S(2)}) %collective-permute-start.12) | collective-permute-done | bytes 196640 | tf_op jit(solution)/shard_map/ppermute | solution.py:135
  244.9 6.6 %reshape.1669 = bf16[2,2,2,2,48,2,1152]{6,5,4,3,2,1,0:T(2,128)(2,1)S(1)} reshape(bf16[768,2304]{1,0:T(8,128)(2,1)} %convolution_convert_fusion.1) | data formatting | bytes 7077888 | tf_op jit(solution)/shard_map/reshape | solution.py:111
  251.5 11.1 %constant_dynamic-slice_fusion.7 = (bf16[2,2,2,2,48,1,1152]{6,5,4,3,2,1,0:T(2,128)(2,1)}, bf16[2,2,2,2,48,1,1152]{6,5,4,3,2,1,0:T(2,128)(2,1)}) fusion(bf16[2,2,2,2,48,2,1152]{6,5,4,3,2,1,0:T(2,128)(2,1)S(1)} %reshape.1669, s32[]{:T(128)S(6)} %select_n.604, s32[]{:T(128)S(6)} %select_n.633), kind=kLoop, calls=%fused_computation.251 | loop fusion | bytes 7077896 | tf_op jit(solution)/shard_map/dynamic-slice
  267.0 5.0 %fusion.21 = (f32[512]{0:T(512)S(1)}, f32[512,768]{1,0:T(8,128)S(1)}) fusion(bf16[512,768]{1,0:T(8,128)(2,1)S(1)} %copy-done.13, f32[512]{0:T(512)S(1)} %broadcast_multiply_fusion.2, f32[768]{0:T(1024)S(1)} %copy-done.53, bf16[512,2304]{0,1:T(8,128)(2,1)} %bitcast.384, bf16[768,2304]{1,0:T(8,128)(2,1)} %bitcast.351), kind=kOutput, calls=%fused_computation.66 | convolution fusion | flops 1813904896 | bytes 8264704 | tf_op jit(solution)/shard_map/tc,dc->td/dot_general | solution.py:321
  294.7 7.3 %collective-permute-start.14 = (bf16[2,2,2,2,48,1152]{5,4,3,2,1,0:T(8,128)(2,1)S(1)}, bf16[2,2,2,2,48,1152]{5,4,3,2,1,0:T(8,128)(2,1)S(1)}, u32[]{:S(2)}, u32[]{:S(2)}) collective-permute-start(bf16[2,2,2,2,48,1152]{5,4,3,2,1,0:T(8,128)(2,1)S(1)} %bitcast.402), channel_id=1, source_target_pairs={{0,2},{2,0},{1,3},{3,1},{4,6},{6,4},{5,7},{7,5},{8,10},{10,8},{9,1... | collective-permute-start | bytes 5308424 | tf_op jit(solution)/shard_map/ppermute | solution.py:81
  314.2 6.0 %collective-permute-start.35 = (bf16[2,2,2,48,384]{4,3,2,1,0:T(8,128)(2,1)S(1)}, bf16[2,2,2,48,384]{4,3,2,1,0:T(8,128)(2,1)S(1)}, u32[]{:S(2)}, u32[]{:S(2)}) collective-permute-start(bf16[2,2,2,48,384]{4,3,2,1,0:T(8,128)(2,1)S(1)} %maximum_select_fusion.23), channel_id=1, source_target_pairs={{0,2},{2,0},{1,3},{3,1},{4,6},{6,4},{5,7},{7,5},{8,10},{10,8},{9,1... | collective-permute-start | bytes 884744 | tf_op jit(solution)/shard_map/ppermute | solution.py:81
  338.5 9.7 %collective-permute-done.56 = bf16[2,2,72,384]{3,2,1,0:T(8,128)(2,1)S(1)} collective-permute-done((bf16[2,2,72,384]{3,2,1,0:T(8,128)(2,1)S(1)}, bf16[2,2,72,384]{3,2,1,0:T(8,128)(2,1)S(1)}, u32[]{:S(2)}, u32[]{:S(2)}) %collective-permute-start.56) | collective-permute-done | bytes 221216 | tf_op jit(solution)/shard_map/ppermute | solution.py:62
  358.2 11.9 %collective-permute-done.15 = bf16[2,2,2,48,1152]{4,3,2,1,0:T(8,128)(2,1)S(1)} collective-permute-done((bf16[2,2,2,48,1152]{4,3,2,1,0:T(8,128)(2,1)S(1)}, bf16[2,2,2,48,1152]{4,3,2,1,0:T(8,128)(2,1)S(1)}, u32[]{:S(2)}, u32[]{:S(2)}) %collective-permute-start.15) | collective-permute-done | bytes 884768 | tf_op jit(solution)/shard_map/ppermute | solution.py:62
  372.5 5.4 %collective-permute-done.16 = bf16[2,2,48,1152]{3,2,1,0:T(8,128)(2,1)S(1)} collective-permute-done((bf16[2,2,48,1152]{3,2,1,0:T(8,128)(2,1)S(1)}, bf16[2,2,48,1152]{3,2,1,0:T(8,128)(2,1)S(1)}, u32[]{:S(2)}, u32[]{:S(2)}) %collective-permute-start.16) | collective-permute-done | bytes 442400 | tf_op jit(solution)/shard_map/ppermute | solution.py:62
  413.0 4.8 %collective-permute-done.45 = bf16[2,2,48,1152]{3,2,1,0:T(8,128)(2,1)S(1)} collective-permute-done((bf16[2,2,48,1152]{3,2,1,0:T(8,128)(2,1)S(1)}, bf16[2,2,48,1152]{3,2,1,0:T(8,128)(2,1)S(1)}, u32[]{:S(2)}, u32[]{:S(2)}) %collective-permute-start.45) | collective-permute-done | bytes 442400 | tf_op jit(solution)/shard_map/ppermute | solution.py:62
  418.0 9.3 %collective-permute-start.46 = (bf16[2,2,2,48,1152]{4,3,2,1,0:T(8,128)(2,1)S(1)}, bf16[2,2,2,48,1152]{4,3,2,1,0:T(8,128)(2,1)S(1)}, u32[]{:S(2)}, u32[]{:S(2)}) collective-permute-start(bf16[2,2,2,48,1152]{4,3,2,1,0:T(8,128)(2,1)S(1)} %maximum_select_fusion.12), channel_id=1, source_target_pairs={{0,2},{2,0},{1,3},{3,1},{4,6},{6,4},{5,7},{7,5},{8,10},{10,8},{9,1... | collective-permute-start | bytes 2654216 | tf_op jit(solution)/shard_map/ppermute | solution.py:81
  (431 shorter events, 256.8 us)
Async XLA Ops:
  0.6 48.7 %collective-permute-start = (bf16[384]{0:T(512)(128)(2,1)}, bf16[384]{0:T(512)(128)(2,1)S(1)}, u32[]{:S(2)}, u32[]{:S(2)}) collective-permute-start(bf16[384]{0:T(512)(128)(2,1)} %param.9), channel_id=1, source_target_pairs={{0,5},{1,4},{4,1},{5,0},{2,7},{3,6},{6,3},{7,2},{8,13},{9,12},{12,... | collective-permute-start | bytes 2312 | tf_op jit(solution)/shard_map/ppermute | solution.py:77
  8.9 39.6 %collective-permute-start.10 = (bf16[288,768]{1,0:T(8,128)(2,1)}, bf16[288,768]{1,0:T(8,128)(2,1)}, u32[]{:S(2)}, u32[]{:S(2)}) collective-permute-start(bf16[288,768]{1,0:T(8,128)(2,1)} %dynamic-slice_bitcast_fusion.7), channel_id=1, source_target_pairs={{0,5},{1,4},{4,1},{5,0},{2,7},{3,6},{6,3},{7,2},{8,13},{9,12},{12,... | collective-permute-start | bytes 1327112 | tf_op jit(solution)/shard_map/ppermute | solution.py:77
  13.7 30.8 %collective-permute-start.1 = (bf16[192,2304]{1,0:T(8,128)(2,1)}, bf16[192,2304]{1,0:T(8,128)(2,1)}, u32[]{:S(2)}, u32[]{:S(2)}) collective-permute-start(bf16[192,2304]{1,0:T(8,128)(2,1)} %dynamic-slice_bitcast_fusion.3), channel_id=1, source_target_pairs={{0,5},{1,4},{4,1},{5,0},{2,7},{3,6},{6,3},{7,2},{8,13},{9,12},{12,... | collective-permute-start | bytes 2654216 | tf_op jit(solution)/shard_map/ppermute | solution.py:77
  13.9 53.2 %collective-permute-start.8 = (bf16[192,2304]{1,0:T(8,128)(2,1)S(1)}, bf16[192,2304]{1,0:T(8,128)(2,1)}, u32[]{:S(2)}, u32[]{:S(2)}) collective-permute-start(bf16[192,2304]{1,0:T(8,128)(2,1)S(1)} %dynamic-slice_bitcast_fusion.2), channel_id=1, source_target_pairs={{0,5},{1,4},{4,1},{5,0},{2,7},{3,6},{6,3},{7,2},{8,13},{9,12},{12,... | collective-permute-start | bytes 2654216 | tf_op jit(solution)/shard_map/ppermute | solution.py:77
  18.6 46.1 %collective-permute-start.6 = (bf16[192,768]{1,0:T(8,128)(2,1)}, bf16[192,768]{1,0:T(8,128)(2,1)S(1)}, u32[]{:S(2)}, u32[]{:S(2)}) collective-permute-start(bf16[192,768]{1,0:T(8,128)(2,1)} %collective-permute-done.5), channel_id=1, source_target_pairs={{0,2},{2,0},{1,3},{3,1},{4,6},{6,4},{5,7},{7,5},{8,10},{10,8},{9,1... | collective-permute-start | bytes 884744 | tf_op jit(solution)/shard_map/ppermute | solution.py:81
  44.5 27.2 %collective-permute-start.2 = (bf16[192,2304]{1,0:T(8,128)(2,1)}, bf16[192,2304]{1,0:T(8,128)(2,1)S(1)}, u32[]{:S(2)}, u32[]{:S(2)}) collective-permute-start(bf16[192,2304]{1,0:T(8,128)(2,1)} %collective-permute-done.1), channel_id=1, source_target_pairs={{0,2},{2,0},{1,3},{3,1},{4,6},{6,4},{5,7},{7,5},{8,10},{10,8},{9,1... | collective-permute-start | bytes 2654216 | tf_op jit(solution)/shard_map/ppermute | solution.py:81
  48.6 20.4 %collective-permute-start.11 = (bf16[288,768]{1,0:T(8,128)(2,1)}, bf16[288,768]{1,0:T(8,128)(2,1)S(1)}, u32[]{:S(2)}, u32[]{:S(2)}) collective-permute-start(bf16[288,768]{1,0:T(8,128)(2,1)} %collective-permute-done.10), channel_id=1, source_target_pairs={{0,2},{2,0},{1,3},{3,1},{4,6},{6,4},{5,7},{7,5},{8,10},{10,8},{9,1... | collective-permute-start | bytes 1327112 | tf_op jit(solution)/shard_map/ppermute | solution.py:81
  49.4 14.1 %collective-permute-start.7 = (bf16[384]{0:T(512)(128)(2,1)S(1)}, bf16[384]{0:T(512)(128)(2,1)S(1)}, u32[]{:S(2)}, u32[]{:S(2)}) collective-permute-start(bf16[384]{0:T(512)(128)(2,1)S(1)} %copy-done.55), channel_id=1, source_target_pairs={{0,5},{1,4},{4,1},{5,0},{2,7},{3,6},{6,3},{7,2},{8,13},{9,12},{12,... | collective-permute-start | bytes 2312 | tf_op jit(solution)/shard_map/ppermute | solution.py:77
  67.1 31.9 %collective-permute-start.9 = (bf16[192,2304]{1,0:T(8,128)(2,1)}, bf16[192,2304]{1,0:T(8,128)(2,1)}, u32[]{:S(2)}, u32[]{:S(2)}) collective-permute-start(bf16[192,2304]{1,0:T(8,128)(2,1)} %collective-permute-done.8), channel_id=1, source_target_pairs={{0,2},{2,0},{1,3},{3,1},{4,6},{6,4},{5,7},{7,5},{8,10},{10,8},{9,1... | collective-permute-start | bytes 2654216 | tf_op jit(solution)/shard_map/ppermute | solution.py:81
  91.5 14.1 %collective-permute-start.4 = (bf16[64,1536]{0,1:T(8,128)(2,1)S(1)}, bf16[64,1536]{0,1:T(8,128)(2,1)S(1)}, u32[]{:S(2)}, u32[]{:S(2)}) collective-permute-start(bf16[64,1536]{0,1:T(8,128)(2,1)S(1)} %get-tuple-element.41), channel_id=1, source_target_pairs={{1,0},{3,2},{5,4},{7,6},{9,8},{11,10},{13,12},{15,14},{17,16},{19,... | collective-permute-start | bytes 589832 | tf_op jit(solution)/shard_map/ppermute | solution.py:27
  92.8 13.7 %collective-permute-start.3 = (bf16[64,1536]{0,1:T(8,128)(2,1)S(1)}, bf16[64,1536]{0,1:T(8,128)(2,1)S(1)}, u32[]{:S(2)}, u32[]{:S(2)}) collective-permute-start(bf16[64,1536]{0,1:T(8,128)(2,1)S(1)} %get-tuple-element.42), channel_id=1, source_target_pairs={{0,1},{2,3},{4,5},{6,7},{8,9},{10,11},{12,13},{14,15},{16,17},{18,... | collective-permute-start | bytes 589832 | tf_op jit(solution)/shard_map/ppermute | solution.py:26
  184.0 78.7 %collective-permute-start.25 = (bf16[2,2,2,2,48,384]{5,4,3,2,1,0:T(8,128)(2,1)}, bf16[2,2,2,2,48,384]{5,4,3,2,1,0:T(8,128)(2,1)}, u32[]{:S(2)}, u32[]{:S(2)}) collective-permute-start(bf16[2,2,2,2,48,384]{5,4,3,2,1,0:T(8,128)(2,1)} %bitcast.346), channel_id=1, source_target_pairs={{0,2},{2,0},{1,3},{3,1},{4,6},{6,4},{5,7},{7,5},{8,10},{10,8},{9,1... | collective-permute-start | bytes 1769480 | tf_op jit(solution)/shard_map/ppermute | solution.py:81
  191.1 96.2 %collective-permute-start.47 = (bf16[2,2,2,2,72,384]{5,4,3,2,1,0:T(8,128)(2,1)}, bf16[2,2,2,2,72,384]{5,4,3,2,1,0:T(8,128)(2,1)}, u32[]{:S(2)}, u32[]{:S(2)}) collective-permute-start(bf16[2,2,2,2,72,384]{5,4,3,2,1,0:T(8,128)(2,1)} %bitcast.343), channel_id=1, source_target_pairs={{0,2},{2,0},{1,3},{3,1},{4,6},{6,4},{5,7},{7,5},{8,10},{10,8},{9,1... | collective-permute-start | bytes 2654216 | tf_op jit(solution)/shard_map/ppermute | solution.py:81
  210.0 114.6 %collective-permute-start.36 = (bf16[2,2,2,2,48,1152]{5,4,0,3,2,1:T(8,128)(2,1)}, bf16[2,2,2,2,48,1152]{5,4,0,3,2,1:T(8,128)(2,1)}, u32[]{:S(2)}, u32[]{:S(2)}) collective-permute-start(bf16[2,2,2,2,48,1152]{5,4,0,3,2,1:T(8,128)(2,1)} %bitcast.338), channel_id=1, source_target_pairs={{0,2},{2,0},{1,3},{3,1},{4,6},{6,4},{5,7},{7,5},{8,10},{10,8},{9,1... | collective-permute-start | bytes 5308424 | tf_op jit(solution)/shard_map/ppermute | solution.py:81
  219.9 14.0 %collective-permute-start.12 = (bf16[64,1536]{0,1:T(8,128)(2,1)S(1)}, bf16[64,1536]{0,1:T(8,128)(2,1)S(1)}, u32[]{:S(2)}, u32[]{:S(2)}) collective-permute-start(bf16[64,1536]{0,1:T(8,128)(2,1)S(1)} %get-tuple-element.25), channel_id=1, source_target_pairs={{1,0},{3,2},{5,4},{7,6},{9,8},{11,10},{13,12},{15,14},{17,16},{19,... | collective-permute-start | bytes 589832 | tf_op jit(solution)/shard_map/ppermute | solution.py:135
  221.3 13.4 %collective-permute-start.13 = (bf16[64,1536]{0,1:T(8,128)(2,1)S(1)}, bf16[64,1536]{0,1:T(8,128)(2,1)S(1)}, u32[]{:S(2)}, u32[]{:S(2)}) collective-permute-start(bf16[64,1536]{0,1:T(8,128)(2,1)S(1)} %get-tuple-element.26), channel_id=1, source_target_pairs={{0,1},{2,3},{4,5},{6,7},{8,9},{10,11},{12,13},{14,15},{16,17},{18,... | collective-permute-start | bytes 589832 | tf_op jit(solution)/shard_map/ppermute | solution.py:135
  289.0 13.1 %collective-permute-start.48 = (bf16[2,2,2,72,384]{4,3,2,1,0:T(8,128)(2,1)S(1)}, bf16[2,2,2,72,384]{4,3,2,1,0:T(8,128)(2,1)S(1)}, u32[]{:S(2)}, u32[]{:S(2)}) collective-permute-start(bf16[2,2,2,72,384]{4,3,2,1,0:T(8,128)(2,1)S(1)} %dynamic-slice_bitcast_fusion.4), channel_id=1, source_target_pairs={{0,8},{8,0},{16,24},{24,16},{2,26},{26,2},{10,18},{18,10},{4,12},{... | collective-permute-start | bytes 1327112 | tf_op jit(solution)/shard_map/ppermute | solution.py:62
  294.7 43.4 %collective-permute-start.14 = (bf16[2,2,2,2,48,1152]{5,4,3,2,1,0:T(8,128)(2,1)S(1)}, bf16[2,2,2,2,48,1152]{5,4,3,2,1,0:T(8,128)(2,1)S(1)}, u32[]{:S(2)}, u32[]{:S(2)}) collective-permute-start(bf16[2,2,2,2,48,1152]{5,4,3,2,1,0:T(8,128)(2,1)S(1)} %bitcast.402), channel_id=1, source_target_pairs={{0,2},{2,0},{1,3},{3,1},{4,6},{6,4},{5,7},{7,5},{8,10},{10,8},{9,1... | collective-permute-start | bytes 5308424 | tf_op jit(solution)/shard_map/ppermute | solution.py:81
  314.2 15.3 %collective-permute-start.35 = (bf16[2,2,2,48,384]{4,3,2,1,0:T(8,128)(2,1)S(1)}, bf16[2,2,2,48,384]{4,3,2,1,0:T(8,128)(2,1)S(1)}, u32[]{:S(2)}, u32[]{:S(2)}) collective-permute-start(bf16[2,2,2,48,384]{4,3,2,1,0:T(8,128)(2,1)S(1)} %maximum_select_fusion.23), channel_id=1, source_target_pairs={{0,2},{2,0},{1,3},{3,1},{4,6},{6,4},{5,7},{7,5},{8,10},{10,8},{9,1... | collective-permute-start | bytes 884744 | tf_op jit(solution)/shard_map/ppermute | solution.py:81
  331.6 26.3 %collective-permute-start.37 = (bf16[2,2,2,48,1152]{4,3,0,2,1:T(8,128)(2,1)S(1)}, bf16[2,2,2,48,1152]{4,3,0,2,1:T(8,128)(2,1)S(1)}, u32[]{:S(2)}, u32[]{:S(2)}) collective-permute-start(bf16[2,2,2,48,1152]{4,3,0,2,1:T(8,128)(2,1)S(1)} %dynamic-slice_bitcast_fusion), channel_id=1, source_target_pairs={{0,8},{8,0},{16,24},{24,16},{2,26},{26,2},{10,18},{18,10},{4,12},{... | collective-permute-start | bytes 2654216 | tf_op jit(solution)/shard_map/ppermute | solution.py:62
  352.3 17.9 %collective-permute-start.15 = (bf16[2,2,2,48,1152]{4,3,2,1,0:T(8,128)(2,1)S(1)}, bf16[2,2,2,48,1152]{4,3,2,1,0:T(8,128)(2,1)S(1)}, u32[]{:S(2)}, u32[]{:S(2)}) collective-permute-start(bf16[2,2,2,48,1152]{4,3,2,1,0:T(8,128)(2,1)S(1)} %dynamic-slice_bitcast_fusion.1), channel_id=1, source_target_pairs={{0,8},{8,0},{16,24},{24,16},{2,26},{26,2},{10,18},{18,10},{4,12},{... | collective-permute-start | bytes 2654216 | tf_op jit(solution)/shard_map/ppermute | solution.py:62
  358.2 12.4 %collective-permute-start.38 = (bf16[2,2,48,1152]{3,2,0,1:T(8,128)(2,1)S(1)}, bf16[2,2,48,1152]{3,2,0,1:T(8,128)(2,1)S(1)}, u32[]{:S(2)}, u32[]{:S(2)}) collective-permute-start(bf16[2,2,48,1152]{3,2,0,1:T(8,128)(2,1)S(1)} %dynamic-slice_bitcast_fusion.5), channel_id=1, source_target_pairs={{0,24},{24,0},{8,16},{16,8},{2,10},{10,2},{18,26},{26,18},{4,28},{... | collective-permute-start | bytes 1327112 | tf_op jit(solution)/shard_map/ppermute | solution.py:62
  410.6 16.9 %collective-permute-start.23 = (bf16[2,2,48,1152]{3,2,1,0:T(8,128)(2,1)S(1)}, bf16[2,2,48,1152]{3,2,1,0:T(8,128)(2,1)S(1)}, u32[]{:S(2)}, u32[]{:S(2)}) collective-permute-start(bf16[2,2,48,1152]{3,2,1,0:T(8,128)(2,1)S(1)} %maximum_select_fusion.17), channel_id=1, source_target_pairs={{0,8},{8,0},{16,24},{24,16},{2,26},{26,2},{10,18},{18,10},{4,12},{... | collective-permute-start | bytes 1327112 | tf_op jit(solution)/shard_map/ppermute | solution.py:62
  418.0 14.5 %collective-permute-start.46 = (bf16[2,2,2,48,1152]{4,3,2,1,0:T(8,128)(2,1)S(1)}, bf16[2,2,2,48,1152]{4,3,2,1,0:T(8,128)(2,1)S(1)}, u32[]{:S(2)}, u32[]{:S(2)}) collective-permute-start(bf16[2,2,2,48,1152]{4,3,2,1,0:T(8,128)(2,1)S(1)} %maximum_select_fusion.12), channel_id=1, source_target_pairs={{0,2},{2,0},{1,3},{3,1},{4,6},{6,4},{5,7},{7,5},{8,10},{10,8},{9,1... | collective-permute-start | bytes 2654216 | tf_op jit(solution)/shard_map/ppermute | solution.py:81
  (95 other events, 584.2 us)
